TPU v7x, 32 devices: a whole 2x2x4 slice. The times are simulated.
32 devices in a mesh: dp: 4 (over z), table: 8 (over y, x, core).
Axes of the slice: x: 2, y: 2, z: 4, core: 2. Of those that a mesh axis runs over, the one named last changes fastest.
Arguments:
- table_rows: float32 [32768, 64], P(('dp', 'table')), may hold values from -0.9 to 0.9
- hot_rows: float32 [2048, 64], replicated, may hold values from -0.9 to 0.9
- bag_ids: int32 [40, 2048], P(None, 'dp'), may hold values from 0 to 32767, as said below
- bag_weights: float32 [40, 2048], P(None, 'dp'), may hold values from 0.5 to 1.5
- items: float32 [64, 2048], P(None, 'dp'), may hold values from -0.75 to 0.75
- labels: int32 [2048], P('dp'), may hold values 0 or 1
- position_of: int32 [32768], replicated, may hold values from 0 to 32767, each once
- hot_ids: int32 [2048], replicated, may hold values from 0 to 32767, as said below
- table_noise: float32 [32768, 64], P(('dp', 'table')), may hold values from -0.12 to 0.12
- hot_noise: float32 [2048, 64], replicated, may hold values from -0.12 to 0.12
Outputs:
- new_table: float32 [32768, 64], P(('dp', 'table'))
- new_hot: float32 [2048, 64], replicated
Inputs may be any that keep to these rules, and one draw needn't show every extreme that they name: `bag_ids`: each draw mixes hot ids and other ids in about equal numbers. `hot_ids`: distinct row ids; ids 0 and 32767 are among them.
All inputs are finite; a program needn't handle non-finite values. No bound on the sum of `labels` on one device may be relied on, other than what follows from the above.
Results may differ from a plain program's by a relative error of at most 0.00007.
Values sent between devices are 32-bit elements; how exact they have to be, the bound alone decides.
A program may use at most 128 MiB of HBM per device.

v0:
```python
import jax
import jax.numpy as jnp
from jax import lax
from jax.sharding import PartitionSpec as P

LEARN_RATE = 20.0
CLIP_NORM = 1.0


def per_device(
    table_rows,
    hot_rows,
    bag_ids,
    bag_weights,
    items,
    labels,
    position_of,
    hot_ids,
    table_noise,
    hot_noise,
):
    shard_rows = table_rows.shape[0]
    width = table_rows.shape[1]
    all_rows = position_of.shape[0]
    hot_count = hot_ids.shape[0]
    examples = bag_ids.shape[1]
    table_count = lax.axis_size("table")
    data_count = lax.axis_size("dp")
    table_index = lax.axis_index("table")
    slot_table = (
        jnp.full((all_rows,), -1, jnp.int32).at[hot_ids].set(jnp.arange(hot_count, dtype=jnp.int32))
    )
    hot_slot = slot_table[bag_ids]
    is_hot = hot_slot >= 0
    safe_slot = jnp.maximum(hot_slot, 0)
    stored_at = position_of[bag_ids]
    owned_mask = jnp.logical_and(
        jnp.logical_not(is_hot), stored_at // shard_rows % table_count == table_index
    )
    owned_weight = jnp.where(owned_mask, bag_weights, 0.0)
    hot_weight = jnp.where(is_hot, bag_weights, 0.0)
    slab_index = stored_at // (shard_rows * table_count) * shard_rows + stored_at % shard_rows
    slab_index = jnp.where(owned_mask, slab_index, 0)
    slab = lax.all_gather(table_rows, "dp", axis=0, tiled=True)
    cold_part = jnp.einsum("jb,jbe->eb", owned_weight, slab[slab_index])
    hot_part = jnp.einsum("jb,jbe->eb", hot_weight, hot_rows[safe_slot])
    equal_ids = (bag_ids[:, None, :] == bag_ids[None, :, :]).astype(jnp.float32)
    pair_weight = bag_weights[:, None, :] * bag_weights[None, :, :] * equal_ids
    owned_pairs = jnp.sum(pair_weight * owned_mask[:, None, :].astype(jnp.float32), axis=(0, 1))
    hot_pairs = jnp.sum(pair_weight * is_hot[:, None, :].astype(jnp.float32), axis=(0, 1))
    pooled_sum, owned_square = lax.psum((cold_part, owned_pairs), "table")
    bag_square = owned_square + hot_pairs
    pooled = pooled_sum + hot_part
    scores = jnp.sum(pooled * items, axis=0)
    residual_term = jax.nn.sigmoid(scores) - labels.astype(jnp.float32)
    grad_vec = residual_term[None, :] * items
    norms = jnp.sqrt(bag_square * jnp.sum(grad_vec * grad_vec, axis=0))
    clipped = grad_vec * (CLIP_NORM / jnp.maximum(norms, CLIP_NORM))[None, :]
    contrib = bag_weights[:, :, None] * clipped.T[None, :, :]
    slab_grad = (
        jnp.zeros((data_count * shard_rows, width), jnp.float32)
        .at[slab_index]
        .add(jnp.where(owned_mask[:, :, None], contrib, 0.0))
    )
    cold_grad = lax.psum_scatter(slab_grad, "dp", scatter_dimension=0, tiled=True)
    new_table = table_rows - LEARN_RATE * (cold_grad + CLIP_NORM * table_noise)
    block_size = examples // table_count
    block_start = table_index * block_size
    block_contrib = lax.dynamic_slice_in_dim(contrib, block_start, block_size, 1)
    block_hot = lax.dynamic_slice_in_dim(is_hot, block_start, block_size, 1)
    block_slot = lax.dynamic_slice_in_dim(safe_slot, block_start, block_size, 1)
    hot_terms = (
        jnp.zeros((hot_count, width), jnp.float32)
        .at[block_slot]
        .add(jnp.where(block_hot[:, :, None], block_contrib, 0.0))
    )
    hot_grad = lax.psum(hot_terms, ("dp", "table"))
    new_hot = hot_rows - LEARN_RATE * (hot_grad + CLIP_NORM * hot_noise)
    return (new_table, new_hot)


def solution(mesh):
    return jax.shard_map(
        per_device,
        mesh=mesh,
        in_specs=(
            P(("dp", "table"), None),
            P(),
            P(None, "dp"),
            P(None, "dp"),
            P(None, "dp"),
            P("dp"),
            P(),
            P(),
            P(("dp", "table"), None),
            P(),
        ),
        out_specs=(P(("dp", "table"), None), P()),
        check_vma=False,
    )
```

profile of v0, /device:TPU:0, one launch (start us, length us, event | category | flops | bytes accessed | tf_op | source)
XLA Modules:
  0.0 677.5 jit_solution(5925432242518259281)
XLA Ops:
  7.2 0.0 copy-start
  7.2 0.0 all-gather.2.cloned.1.call-start
  7.2 2.0 copy.27
  9.2 0.0 all-gather.2.cloned.1.call-update
  9.3 0.0 all-reduce.3.cloned.1.call-start
  9.3 0.9 fusion.15
  10.3 0.0 copy-start.8
  10.3 113.0 %gather_fusion.1 = s32[20480]{0:T(1024)S(1)} fusion(s32[32768]{0:T(1024)S(1)} %copy-done, s32[20480]{0:T(1024)S(1)} %broadcast_clamp_fusion.2), kind=kCustom, calls=%fused_computation.1 | custom fusion | bytes 245760 | tf_op jit(solution)/shard_map/gather | solution.py:36
  123.4 8.1 %scatter_custom_fusion = s32[32768]{0:T(1024)S(1)} fusion(s32[2048]{0:T(1024)S(1)} %compare_select_fusion.3, s32[2048]{0:T(1024)S(1)} %iota.3, s32[]{:T(128)} %constant.69.clone.1), kind=kCustom, calls=%fused_computation.68 | custom fusion | bytes 131076 | tf_op jit(solution)/shard_map/scatter | solution.py:31
  131.5 0.0 copy-start.5
  131.5 0.0 copy-start.2
  131.5 113.0 %gather_fusion = s32[20480]{0:T(1024)S(1)} fusion(s32[32768]{0:T(1024)S(1)} %scatter_custom_fusion, s32[20480]{0:T(1024)S(1)} %broadcast_clamp_fusion.2), kind=kCustom, calls=%fused_computation | custom fusion | bytes 245760 | tf_op jit(solution)/shard_map/gather | solution.py:33
  244.7 0.1 fusion.26
  244.8 0.2 fusion.16
  245.0 0.3 copy.24
  245.4 68.0 %gather_fusion.3 = f32[20480,64]{1,0:T(8,128)} fusion(f32[2048,64]{1,0:T(8,128)S(1)} %copy.24, s32[20480]{0:T(1024)S(1)} %get-tuple-element.13), kind=kCustom, calls=%fused_computation.3 | custom fusion | bytes 10567680 | tf_op jit(solution)/shard_map/gather | solution.py:46
  313.4 6.7 multiply_reduce_fusion
  320.1 0.1 copy.45
  320.2 0.1 compare_select_fusion.2
  320.3 0.1 reshape.284
  320.4 0.9 multiply_reduce_fusion.2
  321.3 15.1 %psum.22 = f32[512]{0:T(512)S(1)} all-reduce(f32[512]{0:T(512)S(1)} %get-tuple-element.7), channel_id=1, replica_groups=mesh['dp'=4,'table'=8] {'table'}, use_global_device_ids=true, to_apply=%region_4.5 | all-reduce | flops 512 | bytes 4096 | tf_op jit(solution)/shard_map/psum | solution.py:51
  336.4 0.0 all-gather.2.cloned.1.call-done
  336.4 69.5 %gather_fusion.2 = f32[20480,64]{1,0:T(8,128)} fusion(f32[4096,64]{1,0:T(8,128)} %all-gather.2.cloned.1.call-done, s32[20480]{0:T(1024)S(1)} %broadcast_clamp_fusion.1), kind=kCustom, calls=%fused_computation.2 | custom fusion | bytes 10567680 | tf_op jit(solution)/shard_map/gather | solution.py:45
  406.0 6.7 multiply_reduce_fusion.1
  412.7 0.8 copy.38
  413.5 0.0 all-reduce.3.cloned.1.call-update
  413.5 0.0 all-reduce.5.cloned.1.call-start
  413.5 0.1 constant_dynamic-slice_fusion
  413.6 52.3 %all-reduce.3.cloned.1.call-done = f32[64,512]{1,0:T(8,128)} async-done(((f32[64,512]{1,0:T(8,128)}), f32[64,512]{1,0:T(8,128)}) %all-reduce.3.cloned.1.call-update) | async-done | bytes 131088 | tf_op jit(solution)/shard_map/psum | solution.py:51
  465.9 0.9 fusion.5
  467.0 0.1 copy.25
  467.1 7.7 %broadcast_multiply_fusion = (f32[40,512,64]{2,1,0:T(8,128)S(1)}, f32[40,512,64]{2,1,0:T(8,128)}) fusion(f32[512,64]{1,0:T(8,128)S(1)} %copy.25, f32[40,512]{1,0:T(8,128)S(1)} %copy-done.2, pred[40,512]{1,0:T(8,128)(4,1)S(1)} %get-tuple-element.9), kind=kLoop, calls=%fused_computation.10 | loop fusion | flops 2621440 | bytes 10719232 | tf_op jit(solution)/shard_map/mul | solution.py:59
  474.8 0.6 dynamic-slice_select_fusion
  475.4 0.0 copy-start.6
  475.4 15.2 %scatter_custom_fusion.2 = f32[2048,64]{1,0:T(8,128)} fusion(s32[2560]{0:T(1024)S(1)} %reshape.284, f32[2560,64]{1,0:T(8,128)S(1)} %bitcast.33, f32[]{:T(128)} %constant.68.clone.1), kind=kCustom, calls=%fused_computation.18 | custom fusion | flops 163840 | bytes 524292 | tf_op jit(solution)/shard_map/scatter-add | solution.py:75
  490.5 0.0 all-reduce.5.cloned.1.call-update
  490.6 0.0 reduce-scatter.2.cloned.1.call-start
  490.6 135.1 %scatter_custom_fusion.1 = f32[4096,64]{1,0:T(8,128)} fusion(s32[20480]{0:T(1024)S(1)} %bitcast.36, f32[20480,64]{1,0:T(8,128)} %bitcast.32, f32[]{:T(128)} %constant.68.clone.1), kind=kCustom, calls=%fused_computation.16 | custom fusion | flops 1310720 | bytes 1049088 | tf_op jit(solution)/shard_map/scatter-add | solution.py:63
  625.7 0.0 reduce-scatter.2.cloned.1.call-update
  625.7 0.3 copy.28
  626.1 0.2 copy.26
  626.3 0.0 all-reduce.5.cloned.1.call-done
  626.3 2.4 multiply_subtract_fusion
  628.7 2.3 copy.31
  631.0 38.0 %reduce-scatter.2.cloned.1.call-done = f32[1024,64]{1,0:T(8,128)} async-done(((f32[4096,64]{1,0:T(8,128)}), f32[1024,64]{1,0:T(8,128)}) %reduce-scatter.2.cloned.1.call-update) | async-done | bytes 262160 | tf_op jit(solution)/shard_map/reduce_scatter | solution.py:65
  669.0 1.1 multiply_subtract_fusion.1
  670.1 0.9 copy.30
  (32 shorter events, 0.3 us)
Async XLA Ops:
  7.2 3.1 copy-start
  7.2 329.2 %all-gather.2.cloned.1.call-start = ((), (), s32[]{:S(2)}) async-start(), calls=%async_computation.1 | async-start | bytes 2621440 | tf_op jit(solution)/shard_map/all_gather | solution.py:44
  9.3 456.7 %all-reduce.3.cloned.1.call-start = ((), (), s32[]{:S(2)}) async-start(), calls=%async_computation.2 | async-start | bytes 262144 | tf_op jit(solution)/shard_map/psum | solution.py:51
  10.3 113.1 %copy-start.8 = (s32[2048]{0:T(1024)S(1)}, s32[2048]{0:T(1024)}, u32[]{:S(2)}) copy-start(s32[2048]{0:T(1024)} %param.17) | copy-start | bytes 24580
  131.5 113.5 %copy-start.5 = (f32[2048,64]{0,1:T(8,128)S(1)}, f32[2048,64]{0,1:T(8,128)}, u32[]{:S(2)}) copy-start(f32[2048,64]{0,1:T(8,128)} %param.11) | copy-start | bytes 1572868
  131.5 113.8 %copy-start.2 = (f32[40,512]{1,0:T(8,128)S(1)}, f32[40,512]{1,0:T(8,128)}, u32[]{:S(2)}) copy-start(f32[40,512]{1,0:T(8,128)} %param.13) | copy-start | bytes 245764
  313.3 7.0 %copy-start.4 = (s32[40,512]{1,0:T(8,128)S(1)}, s32[40,512]{1,0:T(8,128)}, u32[]{:S(2)}) copy-start(s32[40,512]{1,0:T(8,128)} %param.12) | copy-start | bytes 245764
  406.0 60.0 %copy-start.3 = (f32[64,512]{1,0:T(8,128)S(1)}, f32[64,512]{1,0:T(8,128)}, u32[]{:S(2)}) copy-start(f32[64,512]{1,0:T(8,128)} %param.14) | copy-start | bytes 393220
  406.0 60.9 %copy-start.9 = (s32[512]{0:T(512)S(1)}, s32[512]{0:T(512)}, u32[]{:S(2)}) copy-start(s32[512]{0:T(512)} %param.15) | copy-start | bytes 6148
  413.5 212.8 %all-reduce.5.cloned.1.call-start = ((), (), s32[]{:S(2)}) async-start(), calls=%async_computation.4 | async-start | bytes 2097152 | tf_op jit(solution)/shard_map/psum | solution.py:77
  475.4 150.3 %copy-start.6 = (f32[2048,64]{0,1:T(8,128)S(1)}, f32[2048,64]{0,1:T(8,128)}, u32[]{:S(2)}) copy-start(f32[2048,64]{0,1:T(8,128)} %param.19) | copy-start | bytes 1572868
  490.5 135.5 %copy-start.7 = (f32[1024,64]{0,1:T(8,128)S(1)}, f32[1024,64]{0,1:T(8,128)}, u32[]{:S(2)}) copy-start(f32[1024,64]{0,1:T(8,128)} %param.18) | copy-start | bytes 786436
  490.6 178.4 %reduce-scatter.2.cloned.1.call-start = ((), (), s32[]{:S(2)}) async-start(), calls=%async_computation.3 | async-start | bytes 2621440 | tf_op jit(solution)/shard_map/reduce_scatter | solution.py:65
  626.1 42.9 %copy-start.1 = (f32[1024,64]{1,0:T(8,128)S(1)}, f32[1024,64]{1,0:T(8,128)}, u32[]{:S(2)}) copy-start(f32[1024,64]{1,0:T(8,128)} %copy.27) | copy-start | bytes 786436
Sparse Core Ops, SparseCore 0:
  9.6 48.6 all-gather.1
  413.6 52.2 all-reduce.2
  490.7 129.3 all-reduce.4
  625.8 43.0 reduce-scatter.1
where the time goes:
time: 678 us; the launch traced here: 677 us
  local copies, waits for them, and re-layouts  379 us (56%)
  other arithmetic  179 us (26%)
  waiting for transfers between devices  90.4 us (13%)
  blocking collectives  15.1 us (2%)
  between operations  14.1 us (2%)
    scatter-add x1, other arithmetic, per_device(): slab_grad = jnp.zeros((data_count * shard_rows, width), jnp.float32).at[s...  135 us
    gather x3, local copies, waits for them, and re-layouts, per_device(): stored_at = position_of[bag_ids]  113 us
    gather x1, local copies, waits for them, and re-layouts, per_device(): hot_slot = slot_table[bag_ids]  113 us
    gather x1, local copies, waits for them, and re-layouts, per_device(): cold_part = jnp.einsum('jb,jbe->eb', owned_weight, slab[slab_index])  69.5 us
    gather x1, local copies, waits for them, and re-layouts, per_device(): hot_part = jnp.einsum('jb,jbe->eb', hot_weight, hot_rows[safe_slot])  68 us
    psum x1, waiting for transfers between devices, per_device(): pooled_sum, owned_square = lax.psum((cold_part, owned_pairs), 'table')  52.3 us
    reduce_scatter x1, waiting for transfers between devices, per_device(): lax.psum_scatter(slab_grad, 'dp', scatter_dimension=0, tiled=True)  38 us
    scatter-add x1, other arithmetic, per_device(): hot_terms = jnp.zeros((hot_count, width), jnp.float32).at[block_slot].add...  15.2 us
  transfers between devices with their start and end apart: 4, of which 2 were waited for; matrix products, arithmetic and copies ran while one was open for 67% of the time, Pallas kernels for 0%

commit v1 on v0

v1 whole, which is shorter than its diff:
```python
import functools

import jax
import jax.numpy as jnp
from jax import lax
from jax.experimental import pallas as pl
from jax.experimental.pallas import tpu as pltpu
from jax.sharding import PartitionSpec as P

LEARN_RATE = 20.0
CLIP_NORM = 1.0
LOW = 256
MESH = pl.DeviceIdType.MESH
VMEM = pltpu.VMEM
F32, BF16, I32 = jnp.float32, jnp.bfloat16, jnp.int32
NT = (((1,), (1,)), ((), ()))


def dot(a, b):
    return jnp.dot(a, b, preferred_element_type=F32)


def dot_nt(a, b):
    return lax.dot_general(a, b, NT, preferred_element_type=F32)


def split(x):
    high = x.astype(BF16)
    return high, (x - high.astype(F32)).astype(BF16)


def lookup_kernel(
    data_count, planes, pos_ref, hot_ref, ids_ref, w_ref, items_ref, lab_ref, vals_ref, code_ref,
    slots, table, vs, vr, cs, cr,
):
    d = lax.axis_index("dp")
    t = lax.axis_index("table")
    peers = [lax.rem(d + k, data_count) for k in range(1, data_count)]
    barrier = pltpu.get_barrier_semaphore()
    for peer in peers:
        pl.semaphore_signal(barrier, inc=1, device_id=(peer, t), device_id_type=MESH)
    bag, examples = w_ref.shape
    width = items_ref.shape[0]
    vals_ref[d, 0:bag, :] = w_ref[...]
    vals_ref[d, bag : bag + width, :] = items_ref[...]
    vals_ref[d, bag + width : bag + width + 8, :] = jnp.broadcast_to(
        lab_ref[...].astype(F32), (8, examples)
    )
    pl.semaphore_wait(barrier, data_count - 1)

    def send(ref, send_sem, recv_sem):
        copies = []
        for k, peer in enumerate(peers):
            copies.append(
                pltpu.make_async_remote_copy(
                    src_ref=ref.at[d],
                    dst_ref=ref.at[d],
                    send_sem=send_sem.at[k],
                    recv_sem=recv_sem.at[k],
                    device_id=(peer, t),
                    device_id_type=MESH,
                )
            )
            copies[-1].start()
        return copies

    copies = send(vals_ref, vs, vr)

    high_count = pos_ref.shape[0]
    hot_count = hot_ref.shape[1]
    chunk = min(512, hot_count)
    slots[...] = jnp.zeros_like(slots)

    def add_hot(c, _):
        start = pl.multiple_of(c * chunk, chunk)
        hot = hot_ref[:, pl.ds(start, chunk)]
        number = start + 1 + lax.broadcasted_iota(I32, (1, chunk), 1)
        at_high = lax.broadcasted_iota(I32, (high_count, chunk), 0) == hot // LOW
        at_low = lax.broadcasted_iota(I32, (LOW, chunk), 0) == hot % LOW
        low_hot = jnp.where(at_low, 1.0, 0.0).astype(BF16)
        upper = jnp.where(at_high, (number // 256).astype(F32), 0.0).astype(BF16)
        lower = jnp.where(at_high, (number % 256).astype(F32), 0.0).astype(BF16)
        slots[...] += 256.0 * dot_nt(upper, low_hot) + dot_nt(lower, low_hot)
        return 0

    lax.fori_loop(0, hot_count // chunk, add_hot, 0)
    slot = slots[...].astype(I32)
    code = jnp.where(slot > 0, high_count * LOW - 1 + slot, pos_ref[...])
    for p in range(planes):
        part = lax.shift_right_logical(code, 8 * p) & 255
        table[p * high_count : (p + 1) * high_count, :] = part.astype(F32).astype(BF16)

    def look_up(j, _):
        ids = ids_ref[pl.ds(j, 1), :]
        at_low = lax.broadcasted_iota(I32, (LOW, examples), 0) == ids % LOW
        found = dot(table[...], jnp.where(at_low, 1.0, 0.0).astype(BF16))
        at_high = lax.broadcasted_iota(I32, (high_count, examples), 0) == ids // LOW
        total = jnp.zeros((1, examples), F32)
        for p in range(planes):
            part = found[p * high_count : (p + 1) * high_count]
            total += (256.0**p) * jnp.sum(jnp.where(at_high, part, 0.0), axis=0, keepdims=True)
        code_ref[d, pl.ds(j, 1), :] = total.astype(I32)
        return 0

    lax.fori_loop(0, bag, look_up, 0)
    copies += send(code_ref, cs, cr)
    for copy in copies:
        copy.wait()


def weights_kernel(
    table_count, cold_rows, all_rows, vals_ref, code_ref, ext_ref, high_ref, low_ref, sums_ref, acc, ext
):
    mine = lax.axis_index("dp") * table_count + lax.axis_index("table")
    data_count, bag, examples = code_ref.shape
    width = ext_ref.shape[0]
    rows = ext_ref.shape[1]
    hot_rows = rows - cold_rows
    ext[:width, :], ext[width:, :] = split(ext_ref[...])
    lanes = 128
    blocks = examples // lanes
    earlier = (
        lax.broadcasted_iota(I32, (bag, bag), 1) < lax.broadcasted_iota(I32, (bag, bag), 0)
    )
    earlier = jnp.where(earlier, 1.0, 0.0).astype(BF16)

    for d in range(data_count):
        for c in range(blocks):
            here = pl.ds(c * lanes, lanes)
            code = code_ref[d, :, here]
            cold = code - mine * cold_rows
            hot = code - all_rows - mine * hot_rows
            is_cold = (cold >= 0) & (cold < cold_rows) & (code < all_rows)
            is_hot = (hot >= 0) & (hot < hot_rows)
            owned = is_cold | is_hot
            row = jnp.where(is_cold, cold, hot + cold_rows)
            ones = jnp.where(owned, 1.0, 0.0)
            rank = dot(earlier, ones.astype(BF16)).astype(I32)
            rank = jnp.where(owned, rank, -1)
            weight = vals_ref[d, 0:bag, here]
            count = jnp.max(jnp.sum(ones, axis=0, keepdims=True)).astype(I32)
            acc[...] = jnp.zeros_like(acc)
            numbers = lax.broadcasted_iota(I32, (rows, lanes), 0)

            def place(i, _):
                total = acc[...]
                for u in range(2):
                    this = rank == 2 * i + u
                    at = jnp.sum(jnp.where(this, row + 1, 0), axis=0, keepdims=True) - 1
                    w = jnp.sum(jnp.where(this, weight, 0.0), axis=0, keepdims=True)
                    total += jnp.where(numbers == at, w, 0.0)
                acc[...] = total
                return 0

            lax.fori_loop(0, (count + 1) // 2, place, 0)
            total = acc[...]
            high, low = split(total)
            out = pl.ds(d * examples + c * lanes, lanes)
            high_ref[:, out] = high
            low_ref[:, out] = low
            first = dot(ext[...], high)
            pooled = first[:width] + first[width:] + dot(ext[:width, :], low)
            items = vals_ref[d, bag : bag + width, here]
            sums_ref[pl.ds(d, 1), here] = jnp.sum(pooled * items, axis=0, keepdims=True)
            sums_ref[pl.ds(data_count + d, 1), here] = jnp.sum(
                total * total, axis=0, keepdims=True
            )


def update_kernel(
    data_count, table_count, bag, sums_ref, vals_ref, high_ref, low_ref, table_ref, noise_ref,
    hot_ref, hot_noise_ref, new_table_ref, new_hot_ref,
    over_table, over_data, hot_all, clip_all, as_, ar, bs, br, hs, hr, gs, gr,
):
    d = lax.axis_index("dp")
    t = lax.axis_index("table")
    data_peers = [(lax.rem(d + k, data_count), t) for k in range(1, data_count)]
    table_peers = [(d, lax.rem(t + k, table_count)) for k in range(1, table_count)]
    barrier = pltpu.get_barrier_semaphore()
    for peer in data_peers + table_peers:
        pl.semaphore_signal(barrier, inc=1, device_id=peer, device_id_type=MESH)
    pl.semaphore_wait(barrier, data_count + table_count - 2)

    def exchange(ref, at, peers, send_sem, recv_sem):
        copies = []
        for k, peer in enumerate(peers):
            copies.append(
                pltpu.make_async_remote_copy(
                    src_ref=ref.at[at],
                    dst_ref=ref.at[at],
                    send_sem=send_sem.at[k],
                    recv_sem=recv_sem.at[k],
                    device_id=peer,
                    device_id_type=MESH,
                )
            )
            copies[-1].start()
        return copies

    over_table[t] = sums_ref[...]
    for copy in exchange(over_table, t, table_peers, as_, ar):
        copy.wait()
    total = over_table[0]
    for k in range(1, table_count):
        total += over_table[k]
    over_data[d] = total
    for copy in exchange(over_data, d, data_peers, bs, br):
        copy.wait()
    total = over_data[0]
    for k in range(1, data_count):
        total += over_data[k]

    width = table_ref.shape[1]
    examples = sums_ref.shape[1]
    cold_rows = table_ref.shape[0]
    rows = high_ref.shape[0]
    for k in range(data_count):
        items = vals_ref[k, bag : bag + width, :]
        labels = vals_ref[k, bag + width : bag + width + 1, :]
        residual = jax.nn.sigmoid(total[k : k + 1]) - labels
        grad = residual * items
        square = jnp.sum(grad * grad, axis=0, keepdims=True)
        norms = jnp.sqrt(total[data_count + k : data_count + k + 1] * square)
        high, low = split(grad * (CLIP_NORM / jnp.maximum(norms, CLIP_NORM)))
        here = pl.ds(k * examples, examples)
        clip_all[:width, here] = high
        clip_all[width:, here] = low

    def gradient(start, size):
        both = dot_nt(high_ref[pl.ds(start, size), :], clip_all[...])
        rest = dot_nt(low_ref[pl.ds(start, size), :], clip_all[:width, :])
        return both[:, :width] + both[:, width:] + rest

    hot_own = gradient(cold_rows, rows - cold_rows)
    mine = d * table_count + t
    hot_all[mine] = hot_ref[...] - LEARN_RATE * (hot_own + CLIP_NORM * hot_noise_ref[...])
    first = exchange(hot_all, mine, data_peers, hs, hr)

    def update(start, size):
        here = pl.ds(start, size)
        new_table_ref[here, :] = table_ref[here, :] - LEARN_RATE * (
            gradient(start, size) + CLIP_NORM * noise_ref[here, :]
        )

    step = cold_rows // 4
    update(0, step)
    for copy in first:
        copy.wait()
    second = []
    for k in range(data_count):
        at = lax.rem(d + k, data_count) * table_count + t
        second += exchange(hot_all, at, table_peers, gs.at[k], gr.at[k])
    for i in range(1, 4):
        update(i * step, step)
    for copy in second:
        copy.wait()
    new_hot_ref[...] = hot_all[...]


def per_device(
    table_rows,
    hot_rows,
    bag_ids,
    bag_weights,
    items,
    labels,
    position_of,
    hot_ids,
    table_noise,
    hot_noise,
):
    cold_rows, width = table_rows.shape
    all_rows = position_of.shape[0]
    hot_count = hot_ids.shape[0]
    bag, examples = bag_ids.shape
    table_count = lax.axis_size("table")
    data_count = lax.axis_size("dp")
    devices = table_count * data_count
    mine = lax.axis_index("dp") * table_count + lax.axis_index("table")
    hot_own = hot_count // devices
    rows = cold_rows + hot_own
    high_count = all_rows // LOW
    planes = 1
    while 256**planes < all_rows + hot_count:
        planes += 1
    value_rows = bag + width + 8
    limit = 56 * 1024 * 1024
    vmem = pl.BlockSpec(memory_space=VMEM)
    dma = pltpu.SemaphoreType.DMA

    vals, code = pl.pallas_call(
        functools.partial(lookup_kernel, data_count, planes),
        out_shape=(
            jax.ShapeDtypeStruct((data_count, value_rows, examples), F32),
            jax.ShapeDtypeStruct((data_count, bag, examples), I32),
        ),
        in_specs=[vmem] * 6,
        out_specs=(vmem, vmem),
        scratch_shapes=[
            VMEM((high_count, LOW), F32),
            VMEM((planes * high_count, LOW), BF16),
        ]
        + [dma((data_count - 1,))] * 4,
        compiler_params=pltpu.CompilerParams(
            collective_id=0, has_side_effects=True, vmem_limit_bytes=limit
        ),
    )(
        position_of.reshape(high_count, LOW),
        hot_ids.reshape(1, hot_count),
        bag_ids,
        bag_weights,
        items,
        labels.reshape(1, examples),
    )

    hot_mine = lax.dynamic_slice_in_dim(hot_rows, mine * hot_own, hot_own, 0)
    hot_noise_mine = lax.dynamic_slice_in_dim(hot_noise, mine * hot_own, hot_own, 0)
    ext = jnp.concatenate([table_rows, hot_mine], axis=0).T

    high, low, sums = pl.pallas_call(
        functools.partial(weights_kernel, table_count, cold_rows, all_rows),
        out_shape=(
            jax.ShapeDtypeStruct((rows, data_count * examples), BF16),
            jax.ShapeDtypeStruct((rows, data_count * examples), BF16),
            jax.ShapeDtypeStruct((2 * data_count, examples), F32),
        ),
        in_specs=[vmem] * 3,
        out_specs=(vmem, vmem, vmem),
        scratch_shapes=[VMEM((rows, 128), F32), VMEM((2 * width, rows), BF16)],
        compiler_params=pltpu.CompilerParams(vmem_limit_bytes=limit),
    )(vals, code, ext)

    new_table, new_hot = pl.pallas_call(
        functools.partial(update_kernel, data_count, table_count, bag),
        out_shape=(
            jax.ShapeDtypeStruct((cold_rows, width), F32),
            jax.ShapeDtypeStruct((devices, hot_own, width), F32),
        ),
        in_specs=[vmem] * 8,
        out_specs=(vmem, vmem),
        scratch_shapes=[
            VMEM((table_count, 2 * data_count, examples), F32),
            VMEM((data_count, 2 * data_count, examples), F32),
            VMEM((devices, hot_own, width), F32),
            VMEM((2 * width, data_count * examples), BF16),
            dma((table_count - 1,)),
            dma((table_count - 1,)),
            dma((data_count - 1,)),
            dma((data_count - 1,)),
            dma((data_count - 1,)),
            dma((data_count - 1,)),
            dma((data_count, table_count - 1)),
            dma((data_count, table_count - 1)),
        ],
        compiler_params=pltpu.CompilerParams(
            collective_id=1, has_side_effects=True, vmem_limit_bytes=limit
        ),
    )(sums, vals, high, low, table_rows, table_noise, hot_mine, hot_noise_mine)
    return (new_table, new_hot.reshape(hot_count, width))


def solution(mesh):
    return jax.shard_map(
        per_device,
        mesh=mesh,
        in_specs=(
            P(("dp", "table"), None),
            P(),
            P(None, "dp"),
            P(None, "dp"),
            P(None, "dp"),
            P("dp"),
            P(),
            P(),
            P(("dp", "table"), None),
            P(),
        ),
        out_specs=(P(("dp", "table"), None), P()),
        check_vma=False,
    )
```

time: 678 us -> 101 us (0.15)
  local copies, waits for them, and re-layouts: 379 us -> 12 us
  other arithmetic: 179 us -> 1.69 us
  waiting for transfers between devices: 90.4 us -> 0 us
  Pallas kernels: 0 us -> 85.9 us
  blocking collectives: 15.1 us -> 0 us
  between operations: 14.1 us -> 0.66 us
    gather x6 -> x0, local copies, waits for them, and re-layouts: 364 us -> none  [the longest x3 113 us: per_device(): stored_at = position_of[bag_ids]]
    scatter-add x2 -> x0, other arithmetic: 150 us -> none  [the longest x1 135 us: per_device(): slab_grad = jnp.zeros((data_count * shard_rows, width), jnp.float32).at[s...]
    pallas_call x0 -> x3, Pallas kernels: none -> 85.9 us  [the longest x1 33.5 us: per_device(): pl.pallas_call(functools.partial(update_kernel, data_count, table_count,...]
    psum x2 -> x0, waiting for transfers between devices: 52.3 us -> none  [the longest x1 52.3 us: per_device(): pooled_sum, owned_square = lax.psum((cold_part, owned_pairs), 'table')]
    reduce_scatter x1 -> x0, waiting for transfers between devices: 38 us -> none  [per_device(): lax.psum_scatter(slab_grad, 'dp', scatter_dimension=0, tiled=True)]
    psum x1 -> x0, blocking collectives: 15.1 us -> none  [per_device(): pooled_sum, owned_square = lax.psum((cold_part, owned_pairs), 'table')]
    unnamed x5 -> x0, other arithmetic: 14.5 us -> none
    scatter x1 -> x0, local copies, waits for them, and re-layouts: 8.1 us -> none  [per_device(): jnp.full((all_rows,), -1, jnp.int32).at[hot_ids]]
  transfers between devices with their start and end apart: 4 -> 0, of which waited for: 2 -> 0; matrix products, arithmetic and copies ran while one was open for 67% -> 0% of each run, Pallas kernels for 0% -> 0%
where the time goes in v1:
time: 101 us; the launch traced here: 100 us
  Pallas kernels  85.9 us (85%)
  local copies, waits for them, and re-layouts  12 us (12%)
  other arithmetic  1.69 us (2%)
    pallas_call x1, Pallas kernels, per_device(): pl.pallas_call(functools.partial(update_kernel, data_count, table_count,...  33.5 us
    pallas_call x1, Pallas kernels, per_device(): pl.pallas_call(functools.partial(lookup_kernel, data_count, planes), out_...  33.3 us
    pallas_call x1, Pallas kernels, per_device(): pl.pallas_call(functools.partial(weights_kernel, table_count, cold_rows,...  19.1 us
    unnamed x6, local copies, waits for them, and re-layouts  9.55 us

profile of v1, /device:TPU:0, one launch (start us, length us, event | category | flops | bytes accessed | tf_op | source)
XLA Modules:
  0.0 100.2 jit_solution(17968882835395058897)
XLA Ops:
  0.6 0.9 constant_dynamic-slice_fusion
  1.5 0.7 copy.20.hot_noise_ref
  2.2 0.7 copy.19.hot_ref
  2.9 1.6 %reshape.16.pos_ref = s32[128,256]{1,0:T(8,128)} reshape(s32[32768]{0:T(1024)} %param.16) | data formatting | bytes 262144 | tf_op jit(solution)/shard_map/reshape | solution.py:308
  4.5 1.7 %maximum_bitcast_fusion.ext_ref = f32[64,1088]{1,0:T(8,128)} fusion(f32[64,64]{0,1:T(8,128)S(1)} %get-tuple-element.19, f32[1024,64]{0,1:T(8,128)} %param.10), kind=kLoop, calls=%fused_computation | loop fusion | flops 69632 | bytes 557056 | tf_op jit(solution)/shard_map/transpose | solution.py:318
  6.2 2.0 %copy.16.noise_ref = f32[1024,64]{1,0:T(8,128)} copy(f32[1024,64]{0,1:T(8,128)} %param.18) | data formatting | bytes 524288 | tf_op args[8]
  8.1 1.9 %copy.15.table_ref = f32[1024,64]{1,0:T(8,128)} copy(f32[1024,64]{0,1:T(8,128)} %param.10) | data formatting | bytes 524288 | tf_op args[0]
  10.1 33.3 %shard_map.113 = (f32[4,112,512]{2,1,0:T(8,128)}, s32[4,40,512]{2,1,0:T(8,128)}) custom-call(s32[128,256]{1,0:T(8,128)} %reshape.16.pos_ref, s32[1,2048]{1,0:T(1,128)} %bitcast.6, s32[40,512]{1,0:T(8,128)} %ids_ref.1, f32[40,512]{1,0:T(8,128)} %w_ref.1, f32[64,512]{1,0:T(8,128)} %items_ref.1, s32[1,512]{1,0:T(1,128)} %bitcast.7), custom_call_target="tpu_custom_call" | custom-call | tf_op jit(solution)/shard_map/pallas_call | solution.py:291
  43.3 19.1 %shard_map.114 = (bf16[1088,2048]{1,0:T(8,128)(2,1)}, bf16[1088,2048]{1,0:T(8,128)(2,1)}, f32[8,512]{1,0:T(8,128)}) custom-call(f32[4,112,512]{2,1,0:T(8,128)} %get-tuple-element.9.vals_ref, s32[4,40,512]{2,1,0:T(8,128)} %get-tuple-element.10.code_ref, f32[64,1088]{1,0:T(8,128)} %maximum_bitcast_fusion.ext_ref), custom_call_target="tpu_custom_call" | custom-call | tf_op jit(solution)/shard_map/pallas_call | solution.py:320
  62.4 33.5 %shard_map.115 = (f32[1024,64]{1,0:T(8,128)}, f32[32,64,64]{2,1,0:T(8,128)}) custom-call(f32[8,512]{1,0:T(8,128)} %get-tuple-element.11.sums_ref, f32[4,112,512]{2,1,0:T(8,128)} %get-tuple-element.9.vals_ref, bf16[1088,2048]{1,0:T(8,128)(2,1)} %get-tuple-element.12.high_ref, bf16[1088,2048]{1,0:T(8,128)(2,1)} %get-tuple-element.13.low_ref, ...), custom_call_target="tpu_custom_call" | custom-call | tf_op jit(solution)/shard_map/pallas_call | solution.py:333
  95.9 1.9 %copy.17 = f32[1024,64]{0,1:T(8,128)} copy(f32[1024,64]{1,0:T(8,128)} %get-tuple-element.16) | data formatting | bytes 524288
  97.9 2.3 %copy.18 = f32[2048,64]{0,1:T(8,128)} copy(f32[2048,64]{1,0:T(8,128)} %bitcast.5) | data formatting | bytes 1048576

commit v2 on v1

v2 whole, which is shorter than its diff:
```python
import functools

import jax
import jax.numpy as jnp
from jax import lax
from jax.experimental import pallas as pl
from jax.experimental.pallas import tpu as pltpu
from jax.sharding import PartitionSpec as P

LEARN_RATE = 20.0
CLIP_NORM = 1.0
LOW = 128
MESH = pl.DeviceIdType.MESH
VMEM = pltpu.VMEM
F32, BF16, I32 = jnp.float32, jnp.bfloat16, jnp.int32
NT = (((1,), (1,)), ((), ()))


def dot(a, b):
    return jnp.dot(a, b, preferred_element_type=F32)


def dot_nt(a, b):
    return lax.dot_general(a, b, NT, preferred_element_type=F32)


def split(x):
    high = x.astype(BF16)
    return high, (x - high.astype(F32)).astype(BF16)


def remote(ref, at, peer, send_sem, recv_sem):
    copy = pltpu.make_async_remote_copy(
        src_ref=ref.at[at],
        dst_ref=ref.at[at],
        send_sem=send_sem,
        recv_sem=recv_sem,
        device_id=peer,
        device_id_type=MESH,
    )
    copy.start()
    return copy


class Spread:
    def __init__(self, ref, sizes, own, sems):
        self.ref, self.own, self.sems = ref, own, sems
        self.data_count, self.table_count = sizes
        self.d, self.t = lax.axis_index("dp"), lax.axis_index("table")
        self.alike = [
            lax.rem(self.t + 2 * i, self.table_count) for i in range(1, self.table_count // 2)
        ]
        self.partner = self.t + 1 - 2 * lax.rem(self.t, 2)
        self.first, self.second, self.third = [], [], []

    def group(self, k):
        return lax.rem(self.d + self.data_count - k, self.data_count)

    def over_data(self):
        for k in range(1, self.data_count):
            peer = (lax.rem(self.d + k, self.data_count), self.t)
            sems = self.sems[0].at[k], self.sems[1].at[k]
            self.first.append(remote(self.ref, (self.t, self.d), peer, *sems))

    def over_table(self):
        for k in range(0 if self.own else 1, self.data_count):
            if k:
                self.first[k - 1].wait_recv()
            at = (self.t, self.group(k))
            for i, peer in enumerate(self.alike):
                sems = self.sems[2].at[k, i], self.sems[3].at[k, i]
                self.second.append((k, i, remote(self.ref, at, (self.d, peer), *sems)))
            self.to_partner(k, 0)

    def to_partner(self, k, i):
        at = (lax.rem(self.t + self.table_count - 2 * i, self.table_count), self.group(k))
        sems = self.sems[4].at[k, i], self.sems[5].at[k, i]
        self.third.append(remote(self.ref, at, (self.d, self.partner), *sems))

    def over_pair(self):
        for k, i, copy in self.second:
            copy.wait_recv()
            self.to_partner(k, i + 1)

    def finish(self):
        for copy in self.third:
            copy.wait_recv()
        for copy in self.first + [copy for _, _, copy in self.second] + self.third:
            copy.wait_send()


def tile_of(ref, d, tile, lanes=slice(None)):
    per = ref.shape[2] // 8
    return ref[tile // per, d, tile % per * 8 : tile % per * 8 + 8, lanes]


def rows_of(ref, d, start, stop, lanes=slice(None)):
    return jnp.concatenate(
        [tile_of(ref, d, tile, lanes) for tile in range(start // 8, stop // 8)], axis=0
    )


def lookup_kernel(
    data_count, table_count, planes, pos_ref, hot_ref, ids_ref, w_ref, items_ref, lab_ref,
    vals_ref, code_ref, slots, table, *sems,
):
    d = lax.axis_index("dp")
    t = lax.axis_index("table")
    sizes = (data_count, table_count)
    vals = Spread(vals_ref, sizes, False, sems[:6])
    codes = Spread(code_ref, sizes, True, sems[6:])
    barrier = pltpu.get_barrier_semaphore()
    peers = [(lax.rem(d + k, data_count), t) for k in range(1, data_count)]
    peers += [(d, peer) for peer in vals.alike + [vals.partner]]
    for peer in peers:
        pl.semaphore_signal(barrier, inc=1, device_id=peer, device_id_type=MESH)
    bag, examples = w_ref.shape
    width = items_ref.shape[0]
    per = vals_ref.shape[2] // 8
    label = jnp.broadcast_to(lab_ref[...].astype(F32), (8, examples))
    for tile in range(table_count * per):
        start = tile * 8
        if start < bag:
            part = w_ref[start : start + 8, :]
        elif start < bag + width:
            part = items_ref[start - bag : start - bag + 8, :]
        else:
            part = label
        vals_ref[tile // per, d, tile % per * 8 : tile % per * 8 + 8, :] = part
    pl.semaphore_wait(barrier, len(peers))
    vals.over_data()

    high_count = pos_ref.shape[0]
    hot_count = hot_ref.shape[1]
    chunk = min(512, hot_count)
    slots[...] = jnp.zeros_like(slots)

    def add_hot(c, _):
        start = pl.multiple_of(c * chunk, chunk)
        hot = hot_ref[:, pl.ds(start, chunk)]
        number = start + 1 + lax.broadcasted_iota(I32, (1, chunk), 1)
        at_high = lax.broadcasted_iota(I32, (high_count, chunk), 0) == hot // LOW
        at_low = lax.broadcasted_iota(I32, (LOW, chunk), 0) == hot % LOW
        low_hot = jnp.where(at_low, 1.0, 0.0).astype(BF16)
        upper = jnp.where(at_high, (number // 256).astype(F32), 0.0).astype(BF16)
        lower = jnp.where(at_high, (number % 256).astype(F32), 0.0).astype(BF16)
        slots[...] += 256.0 * dot_nt(upper, low_hot) + dot_nt(lower, low_hot)
        return 0

    lax.fori_loop(0, hot_count // chunk, add_hot, 0)
    slot = slots[...].astype(I32)
    code = jnp.where(slot > 0, high_count * LOW - 1 + slot, pos_ref[...])
    for p in range(planes):
        part = lax.shift_right_logical(code, 8 * p) & 255
        table[p * high_count : (p + 1) * high_count, :] = part.astype(F32).astype(BF16)
    vals.over_table()

    mine = pl.multiple_of(jnp.minimum(t, bag // 8 - 1) * 8, 8)

    def look_up(j, _):
        ids = ids_ref[pl.ds(mine + j, 1), :]
        at_low = lax.broadcasted_iota(I32, (LOW, examples), 0) == ids % LOW
        found = dot(table[...], jnp.where(at_low, 1.0, 0.0).astype(BF16))
        at_high = lax.broadcasted_iota(I32, (high_count, examples), 0) == ids // LOW
        total = jnp.zeros((1, examples), F32)
        for p in range(planes):
            part = found[p * high_count : (p + 1) * high_count]
            total += (256.0**p) * jnp.sum(jnp.where(at_high, part, 0.0), axis=0, keepdims=True)
        code_ref[t, d, pl.ds(j, 1), :] = total.astype(I32)
        return 0

    lax.fori_loop(0, 8, look_up, 0)
    codes.over_data()
    vals.over_pair()
    codes.over_table()
    codes.over_pair()
    vals.finish()
    codes.finish()


def weights_kernel(
    sizes, bag, all_rows, vals_ref, code_ref, cold_ref, hot_ref, high_ref, low_ref, sums_ref,
    acc, ext, shares,
):
    data_count, table_count = sizes
    mine = lax.axis_index("dp") * table_count + lax.axis_index("table")
    d = pl.program_id(0)
    examples = code_ref.shape[3]
    width, cold_rows = cold_ref.shape
    hot_rows = hot_ref.shape[1]
    rows = cold_rows + hot_rows
    lanes = 128

    @pl.when(d == 0)
    def _():
        for start, part in ((0, cold_ref[...].T), (cold_rows, hot_ref[...].T)):
            high, low = split(part)
            here = pl.ds(start, part.shape[0])
            ext[here, :width] = high
            ext[here, width : 2 * width] = low
            ext[here, 2 * width :] = high

    earlier = (
        lax.broadcasted_iota(I32, (bag, bag), 1) < lax.broadcasted_iota(I32, (bag, bag), 0)
    )
    earlier = jnp.where(earlier, 1.0, 0.0).astype(BF16)
    high, low = split(rows_of(vals_ref, d, bag, bag + width))
    shares[...] = dot(ext[...], jnp.concatenate([high, high, low], axis=0))

    scores, squares = [], []
    for c in range(examples // lanes):
        here = pl.ds(c * lanes, lanes)
        code = rows_of(code_ref, d, 0, bag, here)
        cold = code - mine * cold_rows
        hot = code - all_rows - mine * hot_rows
        is_cold = (cold >= 0) & (cold < cold_rows) & (code < all_rows)
        is_hot = (hot >= 0) & (hot < hot_rows)
        owned = is_cold | is_hot
        row = jnp.where(is_cold, cold, hot + cold_rows)
        ones = jnp.where(owned, 1.0, 0.0)
        rank = dot(earlier, ones.astype(BF16)).astype(I32)
        rank = jnp.where(owned, rank, -1)
        weight = rows_of(vals_ref, d, 0, bag, here)
        count = jnp.max(jnp.sum(ones, axis=0, keepdims=True)).astype(I32)
        numbers = lax.broadcasted_iota(I32, (rows, lanes), 0)

        def pair(i):
            total = 0.0
            for u in range(2):
                this = rank == 2 * i + u
                at = jnp.sum(jnp.where(this, row + 1, 0), axis=0, keepdims=True) - 1
                w = jnp.sum(jnp.where(this, weight, 0.0), axis=0, keepdims=True)
                total = total + jnp.where(numbers == at, w, 0.0)
            return total

        acc[...] = pair(0)

        def place(i, _):
            acc[...] += pair(i)
            return 0

        lax.fori_loop(1, (count + 1) // 2, place, 0)
        total = acc[...]
        high, low = split(total)
        high_ref[:, here] = high
        low_ref[:, here] = low
        scores.append(jnp.sum(total * shares[:, here], axis=0, keepdims=True))
        squares.append(jnp.sum(total * total, axis=0, keepdims=True))
    sums_ref[pl.ds(d, 1), :] = jnp.concatenate(scores, axis=1)
    sums_ref[pl.ds(data_count + d, 1), :] = jnp.concatenate(squares, axis=1)


def update_kernel(
    data_count, table_count, bag, sums_ref, vals_ref, high_hbm, low_hbm, table_ref, noise_ref,
    hot_ref, hot_noise_ref, new_table_ref, new_hot_ref, high_ref, low_ref,
    over_table, over_data, hot_all, clip_all, load, as_, ar, bs, br, hs, hr, gs, gr,
):
    d = lax.axis_index("dp")
    t = lax.axis_index("table")
    loads = [
        pltpu.make_async_copy(high_hbm, high_ref, load.at[0]),
        pltpu.make_async_copy(low_hbm, low_ref, load.at[1]),
    ]
    data_peers = [(lax.rem(d + k, data_count), t) for k in range(1, data_count)]
    table_peers = [(d, lax.rem(t + k, table_count)) for k in range(1, table_count)]
    barrier = pltpu.get_barrier_semaphore()
    for peer in data_peers + table_peers:
        pl.semaphore_signal(barrier, inc=1, device_id=peer, device_id_type=MESH)
    for copy in loads:
        copy.start()
    pl.semaphore_wait(barrier, data_count + table_count - 2)

    def exchange(ref, at, peers, send_sem, recv_sem):
        return [
            remote(ref, at, peer, send_sem.at[k], recv_sem.at[k]) for k, peer in enumerate(peers)
        ]

    over_table[t] = sums_ref[...]
    for copy in exchange(over_table, t, table_peers, as_, ar):
        copy.wait()
    total = over_table[0]
    for k in range(1, table_count):
        total += over_table[k]
    over_data[d] = total
    for copy in exchange(over_data, d, data_peers, bs, br):
        copy.wait()
    total = over_data[0]
    for k in range(1, data_count):
        total += over_data[k]

    width, cold_rows = table_ref.shape
    examples = sums_ref.shape[1]
    rows = high_ref.shape[0]
    hot_rows = rows - cold_rows
    for k in range(data_count):
        items = rows_of(vals_ref, k, bag, bag + width)
        labels = tile_of(vals_ref, k, (bag + width) // 8)[0:1]
        residual = jax.nn.sigmoid(total[k : k + 1]) - labels
        grad = residual * items
        square = jnp.sum(grad * grad, axis=0, keepdims=True)
        norms = jnp.sqrt(total[data_count + k : data_count + k + 1] * square)
        high, low = split(grad * (CLIP_NORM / jnp.maximum(norms, CLIP_NORM)))
        here = pl.ds(k * examples, examples)
        clip_all[:width, here] = high
        clip_all[width:, here] = low

    for copy in loads:
        copy.wait()

    def gradient(start, size):
        both = dot_nt(clip_all[...], high_ref[pl.ds(start, size), :])
        rest = dot_nt(clip_all[:width, :], low_ref[pl.ds(start, size), :])
        return both[:width] + both[width:] + rest

    hot_own = gradient(cold_rows, hot_rows)
    mine = d * table_count + t
    half = width // 2
    hot_all[mine] = jnp.concatenate([hot_own[:half], hot_own[half:]], axis=1)
    first = exchange(hot_all, mine, data_peers, hs, hr)

    def update(start, size):
        here = pl.ds(start, size)
        new_table_ref[:, here] = table_ref[:, here] - LEARN_RATE * (
            gradient(start, size) + CLIP_NORM * noise_ref[:, here]
        )

    step = cold_rows // 4
    update(0, step)
    for copy in first:
        copy.wait()
    second = []
    for k in range(data_count):
        at = lax.rem(d + k, data_count) * table_count + t
        second += exchange(hot_all, at, table_peers, gs.at[k], gr.at[k])
    for i in range(1, 4):
        update(i * step, step)
    for copy in second:
        copy.wait()
    for pair in range(data_count * table_count // 2):
        here = pl.ds(pair * 2 * hot_rows, 2 * hot_rows)
        left, right = hot_all[2 * pair], hot_all[2 * pair + 1]
        upper = jnp.concatenate([left[:, :hot_rows], right[:, :hot_rows]], axis=1)
        lower = jnp.concatenate([left[:, hot_rows:], right[:, hot_rows:]], axis=1)
        new_hot_ref[:, here] = hot_ref[:, here] - LEARN_RATE * (
            jnp.concatenate([upper, lower], axis=0) + CLIP_NORM * hot_noise_ref[:, here]
        )


def per_device(
    table_rows,
    hot_rows,
    bag_ids,
    bag_weights,
    items,
    labels,
    position_of,
    hot_ids,
    table_noise,
    hot_noise,
):
    cold_rows, width = table_rows.shape
    all_rows = position_of.shape[0]
    hot_count = hot_ids.shape[0]
    bag, examples = bag_ids.shape
    table_count = lax.axis_size("table")
    data_count = lax.axis_size("dp")
    devices = table_count * data_count
    mine = lax.axis_index("dp") * table_count + lax.axis_index("table")
    hot_own = hot_count // devices
    rows = cold_rows + hot_own
    high_count = all_rows // LOW
    planes = 1
    while 256**planes < all_rows + hot_count:
        planes += 1
    tiles = (bag + width) // 8 + 1
    chunk_rows = 8 * (-(-tiles // table_count))
    assert bag // 8 <= table_count and 2 * hot_own == 128 and width == hot_own
    limit = 56 * 1024 * 1024
    vmem = pl.BlockSpec(memory_space=VMEM)
    dma = pltpu.SemaphoreType.DMA
    half = table_count // 2
    spread = [dma((data_count,))] * 2 + [dma((data_count, half))] * 4

    vals, code = pl.pallas_call(
        functools.partial(lookup_kernel, data_count, table_count, planes),
        out_shape=(
            jax.ShapeDtypeStruct((table_count, data_count, chunk_rows, examples), F32),
            jax.ShapeDtypeStruct((table_count, data_count, 8, examples), I32),
        ),
        in_specs=[vmem] * 6,
        out_specs=(vmem, vmem),
        scratch_shapes=[
            VMEM((high_count, LOW), F32),
            VMEM((planes * high_count, LOW), BF16),
        ]
        + spread
        + spread,
        compiler_params=pltpu.CompilerParams(
            collective_id=0, has_side_effects=True, vmem_limit_bytes=limit
        ),
    )(
        position_of.reshape(high_count, LOW),
        hot_ids.reshape(1, hot_count),
        bag_ids,
        bag_weights,
        items,
        labels.reshape(1, examples),
    )

    hot_mine = lax.dynamic_slice_in_dim(hot_rows, mine * hot_own, hot_own, 0)

    def whole(*shape):
        return pl.BlockSpec(shape, lambda d: (0,) * len(shape))

    high, low, sums = pl.pallas_call(
        functools.partial(weights_kernel, (data_count, table_count), bag, all_rows),
        grid=(data_count,),
        out_shape=(
            jax.ShapeDtypeStruct((rows, data_count * examples), BF16),
            jax.ShapeDtypeStruct((rows, data_count * examples), BF16),
            jax.ShapeDtypeStruct((2 * data_count, examples), F32),
        ),
        in_specs=[
            whole(*vals.shape),
            whole(*code.shape),
            whole(width, cold_rows),
            whole(width, hot_own),
        ],
        out_specs=(
            pl.BlockSpec((rows, examples), lambda d: (0, d)),
            pl.BlockSpec((rows, examples), lambda d: (0, d)),
            whole(2 * data_count, examples),
        ),
        scratch_shapes=[
            VMEM((rows, 128), F32),
            VMEM((rows, 3 * width), BF16),
            VMEM((rows, examples), F32),
        ],
        compiler_params=pltpu.CompilerParams(vmem_limit_bytes=limit),
    )(vals, code, table_rows.T, hot_mine.T)

    new_table, new_hot = pl.pallas_call(
        functools.partial(update_kernel, data_count, table_count, bag),
        out_shape=(
            jax.ShapeDtypeStruct((width, cold_rows), F32),
            jax.ShapeDtypeStruct((width, hot_count), F32),
        ),
        in_specs=[vmem] * 2 + [pl.BlockSpec(memory_space=pl.ANY)] * 2 + [vmem] * 4,
        out_specs=(vmem, vmem),
        scratch_shapes=[
            VMEM((rows, data_count * examples), BF16),
            VMEM((rows, data_count * examples), BF16),
            VMEM((table_count, 2 * data_count, examples), F32),
            VMEM((data_count, 2 * data_count, examples), F32),
            VMEM((devices, width // 2, 2 * hot_own), F32),
            VMEM((2 * width, data_count * examples), BF16),
            dma((2,)),
            dma((table_count - 1,)),
            dma((table_count - 1,)),
            dma((data_count - 1,)),
            dma((data_count - 1,)),
            dma((data_count - 1,)),
            dma((data_count - 1,)),
            dma((data_count, table_count - 1)),
            dma((data_count, table_count - 1)),
        ],
        compiler_params=pltpu.CompilerParams(
            collective_id=1, has_side_effects=True, vmem_limit_bytes=limit
        ),
    )(sums, vals, high, low, table_rows.T, table_noise.T, hot_rows.T, hot_noise.T)
    return (new_table.T, new_hot.T)


def solution(mesh):
    return jax.shard_map(
        per_device,
        mesh=mesh,
        in_specs=(
            P(("dp", "table"), None),
            P(),
            P(None, "dp"),
            P(None, "dp"),
            P(None, "dp"),
            P("dp"),
            P(),
            P(),
            P(("dp", "table"), None),
            P(),
        ),
        out_specs=(P(("dp", "table"), None), P()),
        check_vma=False,
    )
```

time: 101 us -> 71.9 us (0.71)
  Pallas kernels: 85.9 us -> 65.9 us
  local copies, waits for them, and re-layouts: 12 us -> 5 us
  other arithmetic: 1.69 us -> 0 us
    pallas_call x1, Pallas kernels: 33.5 us -> 23 us  [per_device(): pl.pallas_call(functools.partial(update_kernel, data_count, table_count,...]
    pallas_call x2, Pallas kernels: 52.4 us -> 42.9 us  [the longest x1 25.1 us: per_device(): pl.pallas_call(functools.partial(lookup_kernel, data_count, table_count,...]
    unnamed x6 -> x2, local copies, waits for them, and re-layouts: 9.55 us -> 3.54 us
    transpose x1 -> x0, other arithmetic: 1.69 us -> none  [per_device(): ext = jnp.concatenate([table_rows, hot_mine], axis=0).T]
    reshape x1 -> x0, local copies, waits for them, and re-layouts: 1.6 us -> none  [per_device(): position_of.reshape(high_count, LOW)]
    transpose x0 -> x1, local copies, waits for them, and re-layouts: none -> 1.45 us  [per_device(): high, low, sums = pl.pallas_call(functools.partial(weights_kernel, (data_...]
where the time goes in v2:
time: 71.9 us; the launch traced here: 71.6 us
  Pallas kernels  65.9 us (92%)
  local copies, waits for them, and re-layouts  5 us (7%)
    pallas_call x1, Pallas kernels, per_device(): pl.pallas_call(functools.partial(lookup_kernel, data_count, table_count,...  25.1 us
    pallas_call x1, Pallas kernels, per_device(): pl.pallas_call(functools.partial(update_kernel, data_count, table_count,...  23 us
    pallas_call x1, Pallas kernels, per_device(): pl.pallas_call(functools.partial(weights_kernel, (data_count, table_count...  17.8 us
    unnamed x2, local copies, waits for them, and re-layouts  3.54 us
    transpose x1, local copies, waits for them, and re-layouts, per_device(): high, low, sums = pl.pallas_call(functools.partial(weights_kernel, (data_...  1.45 us

profile of v2, /device:TPU:0, one launch (start us, length us, event | category | flops | bytes accessed | tf_op | source)
XLA Modules:
  0.0 71.6 jit_solution(12699636055725467744)
XLA Ops:
  0.6 1.5 %dynamic-slice_bitcast_fusion.hot_ref = f32[64,64]{1,0:T(8,128)} fusion(f32[2048,64]{0,1:T(8,128)} %param.11, s32[]{:T(128)S(6)} %select_n.3), kind=kLoop, calls=%fused_computation | loop fusion | bytes 32772 | tf_op jit(solution)/shard_map/transpose | solution.py:440
  2.1 25.1 %shard_map.113 = (f32[8,4,16,512]{3,2,1,0:T(8,128)}, s32[8,4,8,512]{3,2,1,0:T(8,128)}) custom-call(s32[256,128]{1,0:T(8,128)} %bitcast.18, s32[1,2048]{1,0:T(1,128)} %bitcast.19, s32[40,512]{1,0:T(8,128)} %ids_ref.1, f32[40,512]{1,0:T(8,128)} %w_ref.1, f32[64,512]{1,0:T(8,128)} %items_ref.1, s32[1,512]{1,0:T(1,128)} %bitcast.20), custom_call_target="tpu_custom_call" | custom-call | tf_op jit(solution)/shard_map/pallas_call | solution.py:384
  27.2 17.8 %shard_map.114 = (bf16[1088,2048]{1,0:T(8,128)(2,1)}, bf16[1088,2048]{1,0:T(8,128)(2,1)}, f32[8,512]{1,0:T(8,128)}) custom-call(f32[8,4,16,512]{3,2,1,0:T(8,128)} %get-tuple-element.9.vals_ref, s32[8,4,8,512]{3,2,1,0:T(8,128)} %get-tuple-element.10.code_ref, f32[64,1024]{1,0:T(8,128)} %bitcast.11, f32[64,64]{1,0:T(8,128)} %dynamic-slice_bitcast_fusion.hot_ref), custom_call_target="tpu_custom_call" | custom-call | tf_op jit(solution)/shard_map/pallas_call | solution.py:415
  45.0 23.0 %shard_map.115 = (f32[64,1024]{1,0:T(8,128)}, f32[64,2048]{1,0:T(8,128)}) custom-call(f32[8,512]{1,0:T(8,128)} %get-tuple-element.11.sums_ref, f32[8,4,16,512]{3,2,1,0:T(8,128)} %get-tuple-element.9.vals_ref, bf16[1088,2048]{1,0:T(8,128)(2,1)} %get-tuple-element.12.high_hbm, bf16[1088,2048]{1,0:T(8,128)(2,1)} %get-tuple-element.13.low_hbm, ...), custom_call_target="tpu_custom_call" | custom-call | tf_op jit(solution)/shard_map/pallas_call | solution.py:442
  68.0 1.7 %copy.14 = f32[1024,64]{0,1:T(8,128)} copy(f32[1024,64]{0,1:T(8,128)} %bitcast.17) | data formatting | bytes 524288
  69.7 1.9 %copy.15 = f32[2048,64]{0,1:T(8,128)} copy(f32[2048,64]{0,1:T(8,128)} %bitcast.15) | data formatting | bytes 1048576

commit v3 on v2

--- a/solution.py
+++ b/solution.py
@@ -171,8 +171,8 @@
 
     lax.fori_loop(0, 8, look_up, 0)
     codes.over_data()
+    codes.over_table()
     vals.over_pair()
-    codes.over_table()
     codes.over_pair()
     vals.finish()
     codes.finish()
@@ -180,7 +180,7 @@
 
 def weights_kernel(
     sizes, bag, all_rows, vals_ref, code_ref, cold_ref, hot_ref, high_ref, low_ref, sums_ref,
-    acc, ext, shares,
+    acc, ext, shares, at_rank, w_rank,
 ):
     data_count, table_count = sizes
     mine = lax.axis_index("dp") * table_count + lax.axis_index("table")
@@ -207,39 +207,53 @@
     high, low = split(rows_of(vals_ref, d, bag, bag + width))
     shares[...] = dot(ext[...], jnp.concatenate([high, high, low], axis=0))
 
+    code = rows_of(code_ref, d, 0, bag)
+    weight = rows_of(vals_ref, d, 0, bag)
+    cold = code - mine * cold_rows
+    hot = code - all_rows - mine * hot_rows
+    is_cold = (cold >= 0) & (cold < cold_rows) & (code < all_rows)
+    is_hot = (hot >= 0) & (hot < hot_rows)
+    owned = is_cold | is_hot
+    row = jnp.where(is_cold, cold, hot + cold_rows) + 1
+    ones = jnp.where(owned, 1.0, 0.0)
+    rank = dot(earlier, ones.astype(BF16)).astype(I32)
+    rank = jnp.where(owned, rank, -1)
+    blocks = [slice(start, start + lanes) for start in range(0, examples, lanes)]
+    owned_counts = jnp.sum(ones, axis=0, keepdims=True)
+    counts = [jnp.max(owned_counts[:, here]).astype(I32) for here in blocks]
+    most = functools.reduce(jnp.maximum, counts)
+
+    def compact(i, _):
+        for u in range(2):
+            this = rank == 2 * i + u
+            at = jnp.sum(jnp.where(this, row, 0), axis=0, keepdims=True) - 1
+            w = jnp.sum(jnp.where(this, weight, 0.0), axis=0, keepdims=True)
+            for c, here in enumerate(blocks):
+                at_rank[c, pl.ds(2 * i + u, 1), :] = at[:, here]
+                w_rank[c, pl.ds(2 * i + u, 1), :] = w[:, here]
+        return 0
+
+    lax.fori_loop(0, jnp.maximum((most + 1) // 2, 2), compact, 0)
+
+    numbers = lax.broadcasted_iota(I32, (rows, lanes), 0)
     scores, squares = [], []
-    for c in range(examples // lanes):
-        here = pl.ds(c * lanes, lanes)
-        code = rows_of(code_ref, d, 0, bag, here)
-        cold = code - mine * cold_rows
-        hot = code - all_rows - mine * hot_rows
-        is_cold = (cold >= 0) & (cold < cold_rows) & (code < all_rows)
-        is_hot = (hot >= 0) & (hot < hot_rows)
-        owned = is_cold | is_hot
-        row = jnp.where(is_cold, cold, hot + cold_rows)
-        ones = jnp.where(owned, 1.0, 0.0)
-        rank = dot(earlier, ones.astype(BF16)).astype(I32)
-        rank = jnp.where(owned, rank, -1)
-        weight = rows_of(vals_ref, d, 0, bag, here)
-        count = jnp.max(jnp.sum(ones, axis=0, keepdims=True)).astype(I32)
-        numbers = lax.broadcasted_iota(I32, (rows, lanes), 0)
-
-        def pair(i):
+    for c, here in enumerate(blocks):
+
+        def placed(start, number):
             total = 0.0
-            for u in range(2):
-                this = rank == 2 * i + u
-                at = jnp.sum(jnp.where(this, row + 1, 0), axis=0, keepdims=True) - 1
-                w = jnp.sum(jnp.where(this, weight, 0.0), axis=0, keepdims=True)
+            for u in range(number):
+                at = at_rank[c, pl.ds(start + u, 1), :]
+                w = w_rank[c, pl.ds(start + u, 1), :]
                 total = total + jnp.where(numbers == at, w, 0.0)
             return total
 
-        acc[...] = pair(0)
+        acc[...] = placed(0, 4)
 
         def place(i, _):
-            acc[...] += pair(i)
+            acc[...] += placed(2 * i, 2)
             return 0
 
-        lax.fori_loop(1, (count + 1) // 2, place, 0)
+        lax.fori_loop(2, (counts[c] + 1) // 2, place, 0)
         total = acc[...]
         high, low = split(total)
         high_ref[:, here] = high
@@ -251,8 +265,8 @@
 
 
 def update_kernel(
-    data_count, table_count, bag, sums_ref, vals_ref, high_hbm, low_hbm, table_ref, noise_ref,
-    hot_ref, hot_noise_ref, new_table_ref, new_hot_ref, high_ref, low_ref,
+    data_count, table_count, bag, sums_ref, vals_ref, high_hbm, low_hbm, cold_grad_ref, hot_grad_ref,
+    high_ref, low_ref,
     over_table, over_data, hot_all, clip_all, load, as_, ar, bs, br, hs, hr, gs, gr,
 ):
     d = lax.axis_index("dp")
@@ -288,7 +302,7 @@
     for k in range(1, data_count):
         total += over_data[k]
 
-    width, cold_rows = table_ref.shape
+    width, cold_rows = cold_grad_ref.shape
     examples = sums_ref.shape[1]
     rows = high_ref.shape[0]
     hot_rows = rows - cold_rows
@@ -320,9 +334,7 @@
 
     def update(start, size):
         here = pl.ds(start, size)
-        new_table_ref[:, here] = table_ref[:, here] - LEARN_RATE * (
-            gradient(start, size) + CLIP_NORM * noise_ref[:, here]
-        )
+        cold_grad_ref[:, here] = gradient(start, size)
 
     step = cold_rows // 4
     update(0, step)
@@ -341,9 +353,7 @@
         left, right = hot_all[2 * pair], hot_all[2 * pair + 1]
         upper = jnp.concatenate([left[:, :hot_rows], right[:, :hot_rows]], axis=1)
         lower = jnp.concatenate([left[:, hot_rows:], right[:, hot_rows:]], axis=1)
-        new_hot_ref[:, here] = hot_ref[:, here] - LEARN_RATE * (
-            jnp.concatenate([upper, lower], axis=0) + CLIP_NORM * hot_noise_ref[:, here]
-        )
+        hot_grad_ref[:, here] = jnp.concatenate([upper, lower], axis=0)
 
 
 def per_device(
@@ -374,7 +384,7 @@
         planes += 1
     tiles = (bag + width) // 8 + 1
     chunk_rows = 8 * (-(-tiles // table_count))
-    assert bag // 8 <= table_count and 2 * hot_own == 128 and width == hot_own
+    assert bag % 8 == 0 and bag // 8 <= table_count and 2 * hot_own == 128 and width == hot_own
     limit = 56 * 1024 * 1024
     vmem = pl.BlockSpec(memory_space=VMEM)
     dma = pltpu.SemaphoreType.DMA
@@ -435,17 +445,19 @@
             VMEM((rows, 128), F32),
             VMEM((rows, 3 * width), BF16),
             VMEM((rows, examples), F32),
+            VMEM((examples // 128, bag, 128), I32),
+            VMEM((examples // 128, bag, 128), F32),
         ],
         compiler_params=pltpu.CompilerParams(vmem_limit_bytes=limit),
     )(vals, code, table_rows.T, hot_mine.T)
 
-    new_table, new_hot = pl.pallas_call(
+    cold_grad, hot_grad = pl.pallas_call(
         functools.partial(update_kernel, data_count, table_count, bag),
         out_shape=(
             jax.ShapeDtypeStruct((width, cold_rows), F32),
             jax.ShapeDtypeStruct((width, hot_count), F32),
         ),
-        in_specs=[vmem] * 2 + [pl.BlockSpec(memory_space=pl.ANY)] * 2 + [vmem] * 4,
+        in_specs=[vmem] * 2 + [pl.BlockSpec(memory_space=pl.ANY)] * 2,
         out_specs=(vmem, vmem),
         scratch_shapes=[
             VMEM((rows, data_count * examples), BF16),
@@ -467,8 +479,10 @@
         compiler_params=pltpu.CompilerParams(
             collective_id=1, has_side_effects=True, vmem_limit_bytes=limit
         ),
-    )(sums, vals, high, low, table_rows.T, table_noise.T, hot_rows.T, hot_noise.T)
-    return (new_table.T, new_hot.T)
+    )(sums, vals, high, low)
+    new_table = table_rows - LEARN_RATE * (cold_grad.T + CLIP_NORM * table_noise)
+    new_hot = hot_rows - LEARN_RATE * (hot_grad.T + CLIP_NORM * hot_noise)
+    return (new_table, new_hot)
 
 
 def solution(mesh):

time: 71.9 us -> 68.4 us (0.951)
  other arithmetic: 0 us -> 3.62 us
  Pallas kernels: 65.9 us -> 62.3 us
  local copies, waits for them, and re-layouts: 5 us -> 1.47 us
    sub x0 -> x2, other arithmetic: none -> 3.62 us  [the longest x1 1.92 us: per_device(): new_hot = hot_rows - LEARN_RATE * (hot_grad.T + CLIP_NORM * hot_noise)]
    unnamed x2 -> x8, local copies, waits for them, and re-layouts: 3.54 us -> 0.02 us
    pallas_call x1, Pallas kernels: 17.8 us -> 14.7 us  [per_device(): pl.pallas_call(functools.partial(weights_kernel, (data_count, table_count...]
where the time goes in v3:
time: 68.4 us; the launch traced here: 68 us
  Pallas kernels  62.3 us (91%)
  other arithmetic  3.62 us (5%)
  local copies, waits for them, and re-layouts  1.47 us (2%)
    pallas_call x1, Pallas kernels, per_device(): pl.pallas_call(functools.partial(lookup_kernel, data_count, table_count,...  25.1 us
    pallas_call x1, Pallas kernels, per_device(): pl.pallas_call(functools.partial(update_kernel, data_count, table_count,...  22.5 us
    pallas_call x1, Pallas kernels, per_device(): pl.pallas_call(functools.partial(weights_kernel, (data_count, table_count...  14.7 us
    sub x1, other arithmetic, per_device(): new_hot = hot_rows - LEARN_RATE * (hot_grad.T + CLIP_NORM * hot_noise)  1.92 us
    sub x1, other arithmetic, per_device(): table_rows - LEARN_RATE * (cold_grad.T + CLIP_NORM * table_noise)  1.7 us
    transpose x1, local copies, waits for them, and re-layouts, per_device(): high, low, sums = pl.pallas_call(functools.partial(weights_kernel, (data_...  1.45 us

profile of v3, /device:TPU:0, one launch (start us, length us, event | category | flops | bytes accessed | tf_op | source)
XLA Modules:
  0.0 68.0 jit_solution(2011116986096153214)
XLA Ops:
  0.6 1.5 %dynamic-slice_bitcast_fusion.hot_ref = f32[64,64]{1,0:T(8,128)} fusion(f32[2048,64]{0,1:T(8,128)} %param.11, s32[]{:T(128)S(6)} %select_n.3), kind=kLoop, calls=%fused_computation.6 | loop fusion | bytes 32772 | tf_op jit(solution)/shard_map/transpose | solution.py:452
  2.1 25.1 %shard_map.113 = (f32[8,4,16,512]{3,2,1,0:T(8,128)}, s32[8,4,8,512]{3,2,1,0:T(8,128)}) custom-call(s32[256,128]{1,0:T(8,128)} %bitcast.19, s32[1,2048]{1,0:T(1,128)} %bitcast.20, s32[40,512]{1,0:T(8,128)} %ids_ref.1, f32[40,512]{1,0:T(8,128)} %w_ref.1, f32[64,512]{1,0:T(8,128)} %items_ref.1, s32[1,512]{1,0:T(1,128)} %bitcast.21), custom_call_target="tpu_custom_call" | custom-call | tf_op jit(solution)/shard_map/pallas_call | solution.py:394
  27.2 14.7 %shard_map.114 = (bf16[1088,2048]{1,0:T(8,128)(2,1)}, bf16[1088,2048]{1,0:T(8,128)(2,1)}, f32[8,512]{1,0:T(8,128)}) custom-call(f32[8,4,16,512]{3,2,1,0:T(8,128)} %get-tuple-element.9.vals_ref, s32[8,4,8,512]{3,2,1,0:T(8,128)} %get-tuple-element.10.code_ref, f32[64,1024]{1,0:T(8,128)} %bitcast.18, f32[64,64]{1,0:T(8,128)} %dynamic-slice_bitcast_fusion.hot_ref), custom_call_target="tpu_custom_call" | custom-call | tf_op jit(solution)/shard_map/pallas_call | solution.py:425
  41.9 0.0 copy-start
  41.9 0.0 copy-start.3
  41.9 0.0 copy-start.1
  41.9 0.0 copy-start.2
  41.9 22.5 %shard_map.115 = (f32[64,1024]{1,0:T(8,128)}, f32[64,2048]{1,0:T(8,128)}) custom-call(f32[8,512]{1,0:T(8,128)} %get-tuple-element.11.sums_ref, f32[8,4,16,512]{3,2,1,0:T(8,128)} %get-tuple-element.9.vals_ref, bf16[1088,2048]{1,0:T(8,128)(2,1)} %get-tuple-element.12.high_hbm, bf16[1088,2048]{1,0:T(8,128)(2,1)} %get-tuple-element.13.low_hbm), custom_call_target="tpu_custom_call" | custom-call | tf_op jit(solution)/shard_map/pallas_call | solution.py:454
  64.4 0.0 copy-done
  64.4 0.0 copy-done.3
  64.4 1.7 %fusion.3 = f32[1024,64]{0,1:T(8,128)} fusion(f32[1024,64]{0,1:T(8,128)S(1)} %copy-done, f32[1024,64]{0,1:T(8,128)S(1)} %copy-done.3, f32[64,1024]{1,0:T(8,128)} %get-tuple-element.14), kind=kLoop, calls=%fused_computation.5 | loop fusion | flops 196608 | bytes 1048576 | tf_op jit(solution)/shard_map/sub | solution.py:483
  66.1 0.0 copy-done.1
  66.1 0.0 copy-done.2
  66.1 1.9 %fusion.1 = f32[2048,64]{0,1:T(8,128)} fusion(f32[2048,64]{0,1:T(8,128)S(1)} %copy-done.1, f32[2048,64]{0,1:T(8,128)S(1)} %copy-done.2, f32[64,2048]{1,0:T(8,128)} %get-tuple-element.15), kind=kLoop, calls=%fused_computation.2 | loop fusion | flops 393216 | bytes 2097152 | tf_op jit(solution)/shard_map/sub | solution.py:484
Async XLA Ops:
  41.9 22.5 %copy-start = (f32[1024,64]{0,1:T(8,128)S(1)}, f32[1024,64]{0,1:T(8,128)}, u32[]{:S(2)}) copy-start(f32[1024,64]{0,1:T(8,128)} %param.10) | copy-start | bytes 786436
  41.9 22.5 %copy-start.3 = (f32[1024,64]{0,1:T(8,128)S(1)}, f32[1024,64]{0,1:T(8,128)}, u32[]{:S(2)}) copy-start(f32[1024,64]{0,1:T(8,128)} %param.18) | copy-start | bytes 786436
  41.9 24.2 %copy-start.1 = (f32[2048,64]{0,1:T(8,128)S(1)}, f32[2048,64]{0,1:T(8,128)}, u32[]{:S(2)}) copy-start(f32[2048,64]{0,1:T(8,128)} %param.11) | copy-start | bytes 1572868
  41.9 24.2 %copy-start.2 = (f32[2048,64]{0,1:T(8,128)S(1)}, f32[2048,64]{0,1:T(8,128)}, u32[]{:S(2)}) copy-start(f32[2048,64]{0,1:T(8,128)} %param.19) | copy-start | bytes 1572868

commit v4 on v3

--- a/solution.py
+++ b/solution.py
@@ -187,13 +187,16 @@
     d = pl.program_id(0)
     examples = code_ref.shape[3]
     width, cold_rows = cold_ref.shape
-    hot_rows = hot_ref.shape[1]
+    hot_rows = hot_ref.shape[1] // (data_count * table_count)
     rows = cold_rows + hot_rows
     lanes = 128
 
     @pl.when(d == 0)
     def _():
-        for start, part in ((0, cold_ref[...].T), (cold_rows, hot_ref[...].T)):
+        pair = pl.ds(pl.multiple_of(mine // 2 * (2 * hot_rows), 2 * hot_rows), 2 * hot_rows)
+        two = hot_ref[:, pair].T
+        hot_own = jnp.where(mine % 2 == 0, two[:hot_rows], two[hot_rows:])
+        for start, part in ((0, cold_ref[...].T), (cold_rows, hot_own)):
             high, low = split(part)
             here = pl.ds(start, part.shape[0])
             ext[here, :width] = high
@@ -267,7 +270,7 @@
 def update_kernel(
     data_count, table_count, bag, sums_ref, vals_ref, high_hbm, low_hbm, cold_grad_ref, hot_grad_ref,
     high_ref, low_ref,
-    over_table, over_data, hot_all, clip_all, load, as_, ar, bs, br, hs, hr, gs, gr,
+    over_table, over_data, hot_all, clip_all, load, as_, ar, bs, br, *hot_sems,
 ):
     d = lax.axis_index("dp")
     t = lax.axis_index("table")
@@ -327,30 +330,26 @@
         return both[:width] + both[width:] + rest
 
     hot_own = gradient(cold_rows, hot_rows)
-    mine = d * table_count + t
     half = width // 2
-    hot_all[mine] = jnp.concatenate([hot_own[:half], hot_own[half:]], axis=1)
-    first = exchange(hot_all, mine, data_peers, hs, hr)
-
-    def update(start, size):
-        here = pl.ds(start, size)
-        cold_grad_ref[:, here] = gradient(start, size)
-
-    step = cold_rows // 4
-    update(0, step)
-    for copy in first:
-        copy.wait()
-    second = []
-    for k in range(data_count):
-        at = lax.rem(d + k, data_count) * table_count + t
-        second += exchange(hot_all, at, table_peers, gs.at[k], gr.at[k])
-    for i in range(1, 4):
-        update(i * step, step)
-    for copy in second:
-        copy.wait()
+    hot_all[t, d] = jnp.concatenate([hot_own[:half], hot_own[half:]], axis=1)
+    hot = Spread(hot_all, (data_count, table_count), True, hot_sems)
+    hot.over_data()
+
+    def update(i):
+        step = cold_rows // 4
+        cold_grad_ref[:, pl.ds(i * step, step)] = gradient(i * step, step)
+
+    update(0)
+    hot.over_table()
+    update(1)
+    update(2)
+    hot.over_pair()
+    update(3)
+    hot.finish()
     for pair in range(data_count * table_count // 2):
         here = pl.ds(pair * 2 * hot_rows, 2 * hot_rows)
-        left, right = hot_all[2 * pair], hot_all[2 * pair + 1]
+        at = 2 * pair % table_count, 2 * pair // table_count
+        left, right = hot_all[at[0], at[1]], hot_all[at[0] + 1, at[1]]
         upper = jnp.concatenate([left[:, :hot_rows], right[:, :hot_rows]], axis=1)
         lower = jnp.concatenate([left[:, hot_rows:], right[:, hot_rows:]], axis=1)
         hot_grad_ref[:, here] = jnp.concatenate([upper, lower], axis=0)
@@ -375,7 +374,6 @@
     table_count = lax.axis_size("table")
     data_count = lax.axis_size("dp")
     devices = table_count * data_count
-    mine = lax.axis_index("dp") * table_count + lax.axis_index("table")
     hot_own = hot_count // devices
     rows = cold_rows + hot_own
     high_count = all_rows // LOW
@@ -417,8 +415,6 @@
         labels.reshape(1, examples),
     )
 
-    hot_mine = lax.dynamic_slice_in_dim(hot_rows, mine * hot_own, hot_own, 0)
-
     def whole(*shape):
         return pl.BlockSpec(shape, lambda d: (0,) * len(shape))
 
@@ -434,7 +430,7 @@
             whole(*vals.shape),
             whole(*code.shape),
             whole(width, cold_rows),
-            whole(width, hot_own),
+            whole(width, hot_count),
         ],
         out_specs=(
             pl.BlockSpec((rows, examples), lambda d: (0, d)),
@@ -449,7 +445,7 @@
             VMEM((examples // 128, bag, 128), F32),
         ],
         compiler_params=pltpu.CompilerParams(vmem_limit_bytes=limit),
-    )(vals, code, table_rows.T, hot_mine.T)
+    )(vals, code, table_rows.T, hot_rows.T)
 
     cold_grad, hot_grad = pl.pallas_call(
         functools.partial(update_kernel, data_count, table_count, bag),
@@ -464,18 +460,15 @@
             VMEM((rows, data_count * examples), BF16),
             VMEM((table_count, 2 * data_count, examples), F32),
             VMEM((data_count, 2 * data_count, examples), F32),
-            VMEM((devices, width // 2, 2 * hot_own), F32),
+            VMEM((table_count, data_count, width // 2, 2 * hot_own), F32),
             VMEM((2 * width, data_count * examples), BF16),
             dma((2,)),
             dma((table_count - 1,)),
             dma((table_count - 1,)),
             dma((data_count - 1,)),
             dma((data_count - 1,)),
-            dma((data_count - 1,)),
-            dma((data_count - 1,)),
-            dma((data_count, table_count - 1)),
-            dma((data_count, table_count - 1)),
-        ],
+        ]
+        + spread,
         compiler_params=pltpu.CompilerParams(
             collective_id=1, has_side_effects=True, vmem_limit_bytes=limit
         ),

time: 68.4 us -> 66.4 us (0.971)
  local copies, waits for them, and re-layouts: 1.47 us -> 0.02 us
    transpose x1 -> x0, local copies, waits for them, and re-layouts: 1.45 us -> none  [per_device(): high, low, sums = pl.pallas_call(functools.partial(weights_kernel, (data_...]
where the time goes in v4:
time: 66.4 us; the launch traced here: 66.3 us
  Pallas kernels  62 us (93%)
  other arithmetic  3.62 us (5%)
  between operations  0.68 us (1%)
    pallas_call x1, Pallas kernels, per_device(): pl.pallas_call(functools.partial(lookup_kernel, data_count, table_count,...  25.1 us
    pallas_call x1, Pallas kernels, per_device(): pl.pallas_call(functools.partial(update_kernel, data_count, table_count,...  22 us
    pallas_call x1, Pallas kernels, per_device(): pl.pallas_call(functools.partial(weights_kernel, (data_count, table_count...  14.9 us
    sub x1, other arithmetic, per_device(): new_hot = hot_rows - LEARN_RATE * (hot_grad.T + CLIP_NORM * hot_noise)  1.92 us
    sub x1, other arithmetic, per_device(): table_rows - LEARN_RATE * (cold_grad.T + CLIP_NORM * table_noise)  1.7 us

profile of v4, /device:TPU:0, one launch (start us, length us, event | category | flops | bytes accessed | tf_op | source)
XLA Modules:
  0.0 66.3 jit_solution(3508782725200518)
XLA Ops:
  0.6 25.1 %shard_map.113 = (f32[8,4,16,512]{3,2,1,0:T(8,128)}, s32[8,4,8,512]{3,2,1,0:T(8,128)}) custom-call(s32[256,128]{1,0:T(8,128)} %bitcast.19, s32[1,2048]{1,0:T(1,128)} %bitcast.20, s32[40,512]{1,0:T(8,128)} %ids_ref.1, f32[40,512]{1,0:T(8,128)} %w_ref.1, f32[64,512]{1,0:T(8,128)} %items_ref.1, s32[1,512]{1,0:T(1,128)} %bitcast.21), custom_call_target="tpu_custom_call" | custom-call | tf_op jit(solution)/shard_map/pallas_call | solution.py:392
  25.7 14.9 %shard_map.114 = (bf16[1088,2048]{1,0:T(8,128)(2,1)}, bf16[1088,2048]{1,0:T(8,128)(2,1)}, f32[8,512]{1,0:T(8,128)}) custom-call(f32[8,4,16,512]{3,2,1,0:T(8,128)} %get-tuple-element.9.vals_ref, s32[8,4,8,512]{3,2,1,0:T(8,128)} %get-tuple-element.10.code_ref, f32[64,1024]{1,0:T(8,128)} %bitcast.18, f32[64,2048]{1,0:T(8,128)} %bitcast.17), custom_call_target="tpu_custom_call" | custom-call | tf_op jit(solution)/shard_map/pallas_call | solution.py:421
  40.6 0.0 copy-start.1
  40.6 0.0 copy-start.3
  40.6 0.0 copy-start
  40.6 0.0 copy-start.2
  40.6 22.0 %shard_map.115 = (f32[64,1024]{1,0:T(8,128)}, f32[64,2048]{1,0:T(8,128)}) custom-call(f32[8,512]{1,0:T(8,128)} %get-tuple-element.11.sums_ref, f32[8,4,16,512]{3,2,1,0:T(8,128)} %get-tuple-element.9.vals_ref, bf16[1088,2048]{1,0:T(8,128)(2,1)} %get-tuple-element.12.high_hbm, bf16[1088,2048]{1,0:T(8,128)(2,1)} %get-tuple-element.13.low_hbm), custom_call_target="tpu_custom_call" | custom-call | tf_op jit(solution)/shard_map/pallas_call | solution.py:450
  62.7 0.0 copy-done.1
  62.7 0.0 copy-done.3
  62.7 1.7 %fusion.3 = f32[1024,64]{0,1:T(8,128)} fusion(f32[1024,64]{0,1:T(8,128)S(1)} %copy-done.1, f32[1024,64]{0,1:T(8,128)S(1)} %copy-done.3, f32[64,1024]{1,0:T(8,128)} %get-tuple-element.14), kind=kLoop, calls=%fused_computation.5 | loop fusion | flops 196608 | bytes 1048576 | tf_op jit(solution)/shard_map/sub | solution.py:476
  64.4 0.0 copy-done
  64.4 0.0 copy-done.2
  64.4 1.9 %fusion.1 = f32[2048,64]{0,1:T(8,128)} fusion(f32[2048,64]{0,1:T(8,128)S(1)} %copy-done, f32[2048,64]{0,1:T(8,128)S(1)} %copy-done.2, f32[64,2048]{1,0:T(8,128)} %get-tuple-element.15), kind=kLoop, calls=%fused_computation.2 | loop fusion | flops 393216 | bytes 2097152 | tf_op jit(solution)/shard_map/sub | solution.py:477
Async XLA Ops:
  40.6 22.0 %copy-start.1 = (f32[1024,64]{0,1:T(8,128)S(1)}, f32[1024,64]{0,1:T(8,128)}, u32[]{:S(2)}) copy-start(f32[1024,64]{0,1:T(8,128)} %param.10) | copy-start | bytes 786436
  40.6 22.0 %copy-start.3 = (f32[1024,64]{0,1:T(8,128)S(1)}, f32[1024,64]{0,1:T(8,128)}, u32[]{:S(2)}) copy-start(f32[1024,64]{0,1:T(8,128)} %param.18) | copy-start | bytes 786436
  40.6 23.8 %copy-start = (f32[2048,64]{0,1:T(8,128)S(1)}, f32[2048,64]{0,1:T(8,128)}, u32[]{:S(2)}) copy-start(f32[2048,64]{0,1:T(8,128)} %param.11) | copy-start | bytes 1572868
  40.6 23.8 %copy-start.2 = (f32[2048,64]{0,1:T(8,128)S(1)}, f32[2048,64]{0,1:T(8,128)}, u32[]{:S(2)}) copy-start(f32[2048,64]{0,1:T(8,128)} %param.19) | copy-start | bytes 1572868
